TPU v7x, 256 devices: a whole 4x4x8 slice. The times are simulated.
256 devices in a mesh: lm: 16 (over x_lo, z), node: 16 (over x_hi, y, core).
Axes of the slice: x: 4 (x_hi: 2, x_lo: 2; x = x_hi * 2 + x_lo), y: 4, z: 8, core: 2. Of those that a mesh axis runs over, the one named last changes fastest.
Arguments:
- features: bfloat16 [128, 262144], P(None, ('node', 'lm')), may hold values from -6 to 6
- landmarks: bfloat16 [128, 8192], P(None, ('lm', 'node')), may hold values from -6 to 6
- cotangent: bfloat16 [64, 262144], P(None, ('node', 'lm')), may hold values from -24 to 24
- eigen_basis: bfloat16 [64, 8192], P(None, ('lm', 'node')), may hold values from -0.5 to 0.5
- inv_eigen: float32 [64], replicated, may hold values from 0.5 to 8
Outputs:
- grad_features: float32 [128, 262144], P(None, ('node', 'lm'))
- grad_landmarks: float32 [128, 8192], P(None, ('lm', 'node'))
All inputs are finite; a program needn't handle non-finite values.
Results may differ from a plain program's by a relative error of at most 0.004.
Values may be sent and summed in bfloat16 or wider, within the bound.
A program may use at most 64 MiB of HBM per device.

v0:
```python
import jax
import jax.numpy as jnp
from jax import lax
from jax.sharding import PartitionSpec as P


def tile_terms(node_rows, node_grads, marks, marks_square, projection, factor):
    rows_float = node_rows.astype(jnp.float32)
    cross = jnp.dot(node_rows.T, marks, preferred_element_type=jnp.float32)
    rows_square = jnp.sum(rows_float * rows_float, axis=0)
    kernel = jnp.exp(-(rows_square[:, None] + marks_square[None, :] - 2.0 * cross) * (0.5 * factor))
    pull = jnp.dot(node_grads.T, projection, preferred_element_type=jnp.float32)
    weight = pull * kernel
    weight_half = weight.astype(jnp.bfloat16)
    toward = factor * (
        jnp.dot(marks, weight_half.T, preferred_element_type=jnp.float32)
        - rows_float * jnp.sum(weight, axis=1)[None, :]
    )
    backward_term = jnp.dot(node_rows, weight_half, preferred_element_type=jnp.float32)
    column_sums = jnp.sum(weight, axis=0)
    return (toward, backward_term, column_sums)


def per_device(features, landmarks, cotangent, eigen_basis, inv_eigen):
    width = features.shape[0]
    factor = 4.0 / width
    local_projection = (inv_eigen[:, None] * eigen_basis.astype(jnp.float32)).astype(jnp.bfloat16)
    marks, projection = (
        lax.all_gather(landmarks, "node", axis=1, tiled=True),
        lax.all_gather(local_projection, "node", axis=1, tiled=True),
    )
    marks_float = marks.astype(jnp.float32)
    marks_square = jnp.sum(marks_float * marks_float, axis=0)
    group_marks = marks.shape[1]
    group_rows = features.shape[1] * lax.axis_size("lm")
    initial = (
        jnp.zeros((width, group_rows), jnp.float32),
        jnp.zeros((width, group_marks), jnp.float32),
        jnp.zeros((group_marks,), jnp.float32),
    )
    piece_rows = lax.all_gather(features, "lm", axis=1, tiled=True)
    piece_grads = lax.all_gather(cotangent, "lm", axis=1, tiled=True)
    length = piece_rows.shape[1]
    stride = 512

    def advance(state, index):
        buffer, back_total, column_total = state
        offset = index * stride
        node_rows = lax.dynamic_slice_in_dim(piece_rows, offset, stride, 1)
        node_grads = lax.dynamic_slice_in_dim(piece_grads, offset, stride, 1)
        toward, backward_term, column_sums = tile_terms(
            node_rows, node_grads, marks, marks_square, projection, factor
        )
        buffer = lax.dynamic_update_slice_in_dim(buffer, toward, offset, 1)
        return ((buffer, back_total + backward_term, column_total + column_sums), None)

    result, unused = lax.scan(advance, initial, jnp.arange(length // stride, dtype=jnp.int32))
    buffer, back_total, column_total = result
    grad_features = lax.psum_scatter(buffer, "lm", scatter_dimension=1, tiled=True)
    mark_term = factor * (back_total - marks_float * column_total[None, :])
    grad_landmarks = lax.psum_scatter(mark_term, "node", scatter_dimension=1, tiled=True)
    return (grad_features, grad_landmarks)


def solution(mesh):
    return jax.shard_map(
        per_device,
        mesh=mesh,
        in_specs=(
            P(None, ("node", "lm")),
            P(None, ("lm", "node")),
            P(None, ("node", "lm")),
            P(None, ("lm", "node")),
            P(),
        ),
        out_specs=(P(None, ("node", "lm")), P(None, ("lm", "node"))),
        check_vma=False,
    )
```

profile of v0, /device:TPU:1, one launch (start us, length us, event | category | flops | bytes accessed | tf_op | source)
XLA Modules:
  0.0 606.7 jit_solution(15564855085942051826)
XLA Ops:
  7.9 1.8 copy.12
  10.5 26.1 %all_gather.13 = bf16[64,512]{0,1:T(8,128)(2,1)S(1)} all-gather(bf16[64,32]{0,1:T(8,128)(2,1)S(1)} %multiply_convert_fusion), channel_id=1, replica_groups=mesh['lm'=16,'node'=16] {'node'}, dimensions={1}, use_global_device_ids=true | all-gather | bytes 69632 | tf_op jit(solution)/shard_map/all_gather | solution.py:30
  36.7 20.0 %all_gather.15 = bf16[128,512]{0,1:T(8,128)(2,1)S(1)} all-gather(bf16[128,32]{0,1:T(8,128)(2,1)} %param.8), channel_id=1, replica_groups=mesh['lm'=16,'node'=16] {'node'}, dimensions={1}, use_global_device_ids=true | all-gather | bytes 139264 | tf_op jit(solution)/shard_map/all_gather | solution.py:29
  57.0 18.7 %all-gather.3.cloned.1.call-done = bf16[64,16384]{1,0:T(8,128)(2,1)} async-done(((bf16[64,1024]{1,0:T(8,128)(2,1)}), bf16[64,16384]{1,0:T(8,128)(2,1)}) %all-gather.3.cloned.1.call-update) | async-done | bytes 2097168 | tf_op jit(solution)/shard_map/all_gather | solution.py:42
  75.7 77.3 %all-gather.5.cloned.1.call-done = bf16[128,16384]{0,1:T(8,128)(2,1)} async-done(((bf16[128,1024]{0,1:T(8,128)(2,1)}), bf16[128,16384]{0,1:T(8,128)(2,1)}) %all-gather.5.cloned.1.call-update) | async-done | bytes 4194320 | tf_op jit(solution)/shard_map/all_gather | solution.py:41
  152.9 4.1 broadcast_in_dim.6.clone
  157.0 259.7 %while.15 = (s32[]{:T(128)}, f32[128,16384]{1,0:T(8,128)}, f32[128,512]{1,0:T(8,128)S(1)}, f32[512]{0:T(512)S(1)}, s32[32]{0:T(128)S(1)}, /*index=5*/bf16[64,163...) while((s32[]{:T(128)}, f32[128,16384]{1,0:T(8,128)}, ...), condition=%wide.region_5.6_spmd.clone, body=%wide.region_1.5_spmd.clone.sunk | while | flops 237829632 | bytes 6441194 | solution.py:57
  159.3 1.3 fusion.43
  160.6 1.2 fusion.44
  167.4 1.3 fusion.43
  168.7 1.3 fusion.44
  175.6 1.3 fusion.43
  176.8 1.2 fusion.44
  183.6 1.3 fusion.43
  191.8 1.3 fusion.43
  193.0 1.3 fusion.44
  199.9 1.3 fusion.43
  201.1 1.2 fusion.44
  208.0 1.3 fusion.43
  209.2 1.3 fusion.44
  216.1 1.3 fusion.43
  224.2 1.3 fusion.43
  225.4 1.2 fusion.44
  232.3 1.3 fusion.43
  233.5 1.2 fusion.44
  240.4 1.3 fusion.43
  248.5 1.3 fusion.43
  249.8 1.2 fusion.44
  256.6 1.3 fusion.43
  264.7 1.3 fusion.43
  266.0 1.2 fusion.44
  272.9 1.3 fusion.43
  274.1 1.3 fusion.44
  281.0 1.3 fusion.43
  289.1 1.3 fusion.43
  290.4 1.3 fusion.44
  297.2 1.3 fusion.43
  298.5 1.2 fusion.44
  305.4 1.3 fusion.43
  306.6 1.2 fusion.44
  313.5 1.3 fusion.43
  314.8 1.2 fusion.44
  321.7 1.3 fusion.43
  329.8 1.3 fusion.43
  331.0 1.2 fusion.44
  337.9 1.3 fusion.43
  339.1 1.2 fusion.44
  346.0 1.3 fusion.43
  347.3 1.2 fusion.44
  354.1 1.3 fusion.43
  355.4 1.3 fusion.44
  362.2 1.3 fusion.43
  370.3 1.3 fusion.43
  378.4 1.3 fusion.43
  379.7 1.2 fusion.44
  386.5 1.3 fusion.43
  387.8 1.2 fusion.44
  394.7 1.3 fusion.43
  402.8 1.3 fusion.43
  404.1 1.2 fusion.44
  410.9 1.3 fusion.43
  412.2 1.2 fusion.44
  418.3 76.7 %reduce-scatter.5.cloned.1.call-done = f32[128,32]{0,1:T(8,128)} async-done(((f32[128,512]{0,1:T(8,128)}), f32[128,32]{0,1:T(8,128)}) %reduce-scatter.5.cloned.1.call-update) | async-done | bytes 16400 | tf_op jit(solution)/shard_map/reduce_scatter | solution.py:61
  495.0 105.2 %reduce-scatter.3.cloned.1.call-done = f32[128,1024]{1,0:T(8,128)} async-done(((f32[128,16384]{1,0:T(8,128)}), f32[128,1024]{1,0:T(8,128)}) %reduce-scatter.3.cloned.1.call-update) | async-done | bytes 524304 | tf_op jit(solution)/shard_map/reduce_scatter | solution.py:59
  (250 shorter events, 171.9 us)
Async XLA Ops:
  7.2 68.5 %all-gather.3.cloned.1.call-start = ((), (), s32[]{:S(2)}) async-start(), calls=%async_computation.2 | async-start | bytes 2228224 | tf_op jit(solution)/shard_map/all_gather | solution.py:42
  7.9 145.0 %all-gather.5.cloned.1.call-start = ((), (), s32[]{:S(2)}) async-start(), calls=%async_computation.3 | async-start | bytes 4456448 | tf_op jit(solution)/shard_map/all_gather | solution.py:41
  9.8 485.2 %reduce-scatter.5.cloned.1.call-start = ((), (), s32[]{:S(2)}) async-start(), calls=%async_computation.5 | async-start | bytes 278528 | tf_op jit(solution)/shard_map/reduce_scatter | solution.py:61
  417.7 182.4 %reduce-scatter.3.cloned.1.call-start = ((), (), s32[]{:S(2)}) async-start(), calls=%async_computation.4 | async-start | bytes 8912896 | tf_op jit(solution)/shard_map/reduce_scatter | solution.py:59
Sparse Core Ops, SparseCore 0:
  9.8 65.8 all-gather.2
  78.0 74.8 all-gather.4
  417.8 77.0 reduce-scatter.4
  497.9 102.1 reduce-scatter.2
where the time goes:
time: 611 us; the launch traced here: 607 us
  waiting for transfers between devices  279 us (46%)
  matrix products  157 us (26%)
  local copies, waits for them, and re-layouts  52.6 us (9%)
  blocking collectives  46 us (8%)
  other arithmetic  35.8 us (6%)
  loops' own time  22.1 us (4%)
  between operations  13.8 us (2%)
    reduce_scatter x1, waiting for transfers between devices, per_device(): lax.psum_scatter(buffer, 'lm', scatter_dimension=1, tiled=True)  105 us
    all_gather x1, waiting for transfers between devices, per_device(): piece_rows = lax.all_gather(features, 'lm', axis=1, tiled=True)  77.3 us
    reduce_scatter x1, waiting for transfers between devices, per_device(): lax.psum_scatter(mark_term, 'node', scatter_dimension=1, tiled=True)  76.7 us
    dot_general x32, matrix products, tile_terms(): cross = jnp.dot(node_rows.T, marks, preferred_element_type=jnp.float32)  40.4 us
    dot_general x32, matrix products, tile_terms(): pull = jnp.dot(node_grads.T, projection, preferred_element_type=jnp.float32)  40 us
    dot_general x32, matrix products, tile_terms(): jnp.dot(marks, weight_half.T, preferred_element_type=jnp.float32)  38.8 us
    dot_general x32, matrix products, tile_terms(): jnp.dot(node_rows, weight_half, preferred_element_type=jnp.float32)  38 us
    reduce_sum x32, other arithmetic, tile_terms(): rows_square = jnp.sum(rows_float * rows_float, axis=0)  33.8 us
  transfers between devices with their start and end apart: 4, of which 4 were waited for; matrix products, arithmetic and copies ran while one was open for 0% of the time, Pallas kernels for 0%

commit v1 on v0

v1 whole, which is shorter than its diff:
```python
import functools
import math

import jax
import jax.numpy as jnp
from jax import lax
from jax.experimental import pallas as pl
from jax.experimental.pallas import tpu as pltpu
from jax.sharding import PartitionSpec as P

MESH = pl.DeviceIdType.MESH
F32 = jnp.float32
BF16 = jnp.bfloat16
LAST = (((1,), (1,)), ((), ()))
ORDER = (1, 3, 2)
PASS = 512


def coordinates():
    lm, node = lax.axis_index("lm"), lax.axis_index("node")
    x, y, z, core = (lm // 8) + 2 * (node // 8), (node // 2) % 4, lm % 8, node % 2
    first = x * (1 - core) + y * core
    second = y * (1 - core) + x * core
    return first, second, z, core


def device(first, second, z, core, other=0):
    x = first * (1 - core) + second * core
    y = second * (1 - core) + first * core
    side = core * (1 - other) + (1 - core) * other
    return {"lm": (x % 2) * 8 + z, "node": (x // 2 * 4 + y) * 2 + side}


def pieces(rows, ones_first):
    square = jnp.sum(rows * rows, axis=1, keepdims=True) * -0.5
    high = square.astype(BF16).astype(F32)
    rest = square - high
    middle = rest.astype(BF16).astype(F32)
    low = rest - middle
    lane = lax.broadcasted_iota(jnp.int32, rows.shape, 1)
    at = 3 if ones_first else 0
    one = 0 if ones_first else 3
    zero = jnp.zeros(rows.shape, F32)
    out = jnp.where((lane >= one) & (lane < one + 3), 1.0, zero)
    out = jnp.where(lane == at, high, out)
    out = jnp.where(lane == at + 1, middle, out)
    out = jnp.where(lane == at + 2, low, out)
    return out.astype(BF16)


def kernel(
    factor, x_ref, l_ref, g_ref, e_ref, inv_ref, gf_ref, gl_ref,
    marks, mate_x, mate_g, rows, grads, wide, weights,
    send1, recv1, own, send2, recv2, send3, recv3, back, mate_back, mine,
    z_s, z_r, c_s, c_r, g_s, g_r, r1_s, r1_r, r2_s, r2_r, r3_s, r3_r, t_s, t_r,
):
    first, second, z, core = coordinates()
    half = x_ref.shape[1]

    def on_first(step):
        return device((first + step) % 4, second, z, core)

    def on_second(step):
        return device(first, (second + step) % 4, z, core)

    def on_z(step):
        return device(first, second, (z + step) % 8, core)

    mate = device(first, second, z, core, 1)

    def remote(src, dst, s, r, to):
        return pltpu.make_async_remote_copy(
            src_ref=src, dst_ref=dst, send_sem=s, recv_sem=r, device_id=to, device_id_type=MESH
        )

    barrier = pltpu.get_barrier_semaphore()
    partners = [on_z(d) for d in range(1, 8)]
    partners += [on_first(d) for d in range(1, 4)] + [on_second(d) for d in range(1, 4)] + [mate]
    for partner in partners:
        pl.semaphore_signal(barrier, inc=1, device_id=partner, device_id_type=MESH)

    at = pl.ds(pl.multiple_of(z * 16, 16), 16)
    own_rows = l_ref[...].astype(F32).T
    marks[0, 0, at, :] = own_rows[:16].astype(BF16)
    marks[0, 1, at, :] = own_rows[16:].astype(BF16)
    projection = e_ref[...].astype(F32).T * inv_ref[...]
    marks[0, 2, at, :] = jnp.concatenate([projection[:16], projection[16:]], axis=1).astype(BF16)

    pl.semaphore_wait(barrier, len(partners))
    sent = []

    def go(copy):
        copy.start()
        sent.append(copy)
        return copy

    z_in = [go(remote(marks.at[0, :, at, :], marks.at[0, :, at, :], z_s.at[d], z_r.at[d], on_z(d + 1))) for d in range(7)]
    x_in = go(remote(x_ref, mate_x, c_s.at[0], c_r.at[0], mate))
    g_in = go(remote(g_ref, mate_g, c_s.at[1], c_r.at[1], mate))

    def prepare(x, g, base):
        turned = x[...].astype(F32).T
        rows[base : base + half, :128] = turned.astype(BF16)
        rows[base : base + half, 128:] = pieces(turned, False)
        pulled = g[...].astype(F32).T
        grads[base : base + half, :] = jnp.concatenate([pulled, pulled], axis=1).astype(BF16)
        wide[:128, base : base + half] = x[...]

    prepare(x_ref, g_ref, 0)
    wide[128:, :] = (lax.broadcasted_iota(jnp.int32, (16, 2 * half), 0) == 0).astype(F32).astype(BF16)
    x_in.wait_recv()
    g_in.wait_recv()
    prepare(mate_x, mate_g, half)

    scale = factor * math.log2(math.e)

    def mark_rows(k):
        return marks[k, 0:2].reshape(256, 128)

    def weigh(k):
        plain = mark_rows(k)
        near = jnp.concatenate([plain, pieces(plain.astype(F32), True)], axis=1)
        packed = marks[k, 2]
        lane = lax.broadcasted_iota(jnp.int32, packed.shape, 1)
        zero = jnp.zeros_like(packed)
        pull = jnp.concatenate([jnp.where(lane < 64, packed, zero), jnp.where(lane < 64, zero, packed)], axis=0)
        cross = lax.dot_general(rows[...], near, LAST, preferred_element_type=F32)
        pulled = lax.dot_general(grads[...], pull, LAST, preferred_element_type=F32)
        weights[k] = (pulled * jnp.exp2(cross * scale)).astype(BF16)

    def backward(k):
        total = jnp.dot(wide[...], weights[k], preferred_element_type=F32).T
        return total[:, :128] - mark_rows(k).astype(F32) * total[:, 128:129]

    for c in z_in:
        c.wait_recv()
    incoming = {}
    for d in range(1, 4):
        incoming[d] = go(remote(marks.at[0], marks.at[d], g_s.at[d], g_r.at[d], on_first(-d + 4)))
    for d in ORDER:
        incoming[4 * d] = go(remote(marks.at[0], marks.at[4 * d], g_s.at[4 * d], g_r.at[4 * d], on_second(-d + 4)))
    weigh(0)
    for k in ORDER:
        incoming[k].wait_recv()
        for d in ORDER:
            s = 4 * d + k
            incoming[s] = go(remote(marks.at[k], marks.at[s], g_s.at[s], g_r.at[s], on_second(-d + 4)))
    for k in ORDER:
        weigh(k)

    reduce1 = []
    ready = []
    behind = None

    def ship():
        for k in ready:
            d, f = k // 4, k % 4
            n = (d - 1) * 4 + f
            reduce1.append(go(remote(send1.at[n], recv1.at[n], r1_s.at[n], r1_r.at[n], on_second(d))))
        ready.clear()

    def finish(k):
        send1[(k // 4 - 1) * 4 + k % 4] = backward(k).astype(BF16)
        ready.append(k)

    for d in ORDER:
        ship()
        for f in range(4):
            incoming[4 * d + f].wait_recv()
        for f in range(4):
            weigh(4 * d + f)
            if behind is not None:
                finish(behind)
            behind = 4 * d + f
    finish(behind)
    ship()
    for f in range(4):
        own[f] = backward(f)

    ones = (lax.broadcasted_iota(jnp.int32, (256, 128), 1) == 0).astype(F32).astype(BF16)

    def toward(r):
        total = jnp.zeros((PASS, 256), F32)
        for k in range(16):
            total = total + jnp.dot(
                weights[k, r : r + PASS, :], jnp.concatenate([mark_rows(k), ones], axis=1), preferred_element_type=F32
            )
        return total[:, :128] - rows[r : r + PASS, :128].astype(F32) * total[:, 128:129]

    for r in range(0, half, PASS):
        if r == PASS:
            for c in reduce1:
                c.wait_recv()
            reduce2 = []
            for f in (1, 3, 2, 0):
                total = own[f]
                for d in range(3):
                    total = total + recv1[d * 4 + f].astype(F32)
                if f:
                    send2[f - 1] = total
                    reduce2.append(go(remote(send2.at[f - 1], recv2.at[f - 1], r2_s.at[f - 1], r2_r.at[f - 1], on_first(f))))
                else:
                    own[0] = total
        back[r : r + PASS, :] = toward(half + r)
    t_in = go(remote(back, mate_back, t_s, t_r, mate))
    for r in range(0, half, PASS):
        if r == PASS:
            for c in reduce2:
                c.wait_recv()
            total = own[0] + recv2[0] + recv2[1] + recv2[2]
            send3[...] = total.reshape(2, 128, 128)
            reduce3 = []
            for d in range(7):
                to = (z + d + 1) % 8
                part = pl.ds(pl.multiple_of(to * 16, 16), 16)
                reduce3.append(go(remote(send3.at[:, part, :], recv3.at[d], r3_s.at[d], r3_r.at[d], on_z(d + 1))))
        mine[r : r + PASS, :] = toward(r)

    t_in.wait_recv()
    gf_ref[...] = factor * (mine[...] + mate_back[...]).T

    for c in reduce3:
        c.wait_recv()
    total = send3[:, at, :]
    for d in range(7):
        total = total + recv3[d]
    gl_ref[...] = factor * total.reshape(32, 128).T
    for c in sent:
        c.wait_send()


def per_device(features, landmarks, cotangent, eigen_basis, inv_eigen):
    width, count = features.shape
    vmem = pl.BlockSpec(memory_space=pltpu.VMEM)
    dma = pltpu.SemaphoreType.DMA
    return pl.pallas_call(
        functools.partial(kernel, 4.0 / width),
        out_shape=(
            jax.ShapeDtypeStruct(features.shape, F32),
            jax.ShapeDtypeStruct(landmarks.shape, F32),
        ),
        in_specs=[vmem] * 5,
        out_specs=(vmem, vmem),
        scratch_shapes=[
            pltpu.VMEM((16, 3, 128, 128), BF16),
            pltpu.VMEM((128, count), BF16),
            pltpu.VMEM((64, count), BF16),
            pltpu.VMEM((2 * count, 256), BF16),
            pltpu.VMEM((2 * count, 128), BF16),
            pltpu.VMEM((144, 2 * count), BF16),
            pltpu.VMEM((16, 2 * count, 256), BF16),
            pltpu.VMEM((12, 256, 128), BF16),
            pltpu.VMEM((12, 256, 128), BF16),
            pltpu.VMEM((4, 256, 128), F32),
            pltpu.VMEM((3, 256, 128), F32),
            pltpu.VMEM((3, 256, 128), F32),
            pltpu.VMEM((2, 128, 128), F32),
            pltpu.VMEM((7, 2, 16, 128), F32),
            pltpu.VMEM((count, 128), F32),
            pltpu.VMEM((count, 128), F32),
            pltpu.VMEM((count, 128), F32),
            dma((7,)), dma((7,)), dma((2,)), dma((2,)), dma((16,)), dma((16,)),
            dma((12,)), dma((12,)), dma((3,)), dma((3,)), dma((7,)), dma((7,)), dma, dma,
        ],
        compiler_params=pltpu.CompilerParams(
            collective_id=0, has_side_effects=True, vmem_limit_bytes=60 * 2**20
        ),
    )(features, landmarks, cotangent, eigen_basis, inv_eigen.reshape(1, -1))


def solution(mesh):
    return jax.shard_map(
        per_device,
        mesh=mesh,
        in_specs=(
            P(None, ("node", "lm")),
            P(None, ("lm", "node")),
            P(None, ("node", "lm")),
            P(None, ("lm", "node")),
            P(),
        ),
        out_specs=(P(None, ("node", "lm")), P(None, ("lm", "node"))),
        check_vma=False,
    )
```

time: 611 us -> 67.2 us (0.11)
  the two profiles are of different devices: /device:TPU:1 before, /device:TPU:6 now
where the time goes in v1:
time: 67.2 us; the launch traced here: 66.9 us
  Pallas kernels  60.8 us (90%)
  local copies, waits for them, and re-layouts  5.52 us (8%)
    pallas_call x1, Pallas kernels, per_device(): pl.pallas_call(functools.partial(kernel, 4.0 / width), out_shape=(jax.Sha...  60.8 us
    unnamed x5, local copies, waits for them, and re-layouts  4 us
    pallas_call x1, local copies, waits for them, and re-layouts, per_device(): pl.pallas_call(functools.partial(kernel, 4.0 / width), out_shape=(jax.Sha...  1.52 us

profile of v1, /device:TPU:6, one launch (start us, length us, event | category | flops | bytes accessed | tf_op | source)
XLA Modules:
  0.0 66.9 jit_solution(8547460426423738856)
XLA Ops:
  0.6 0.0 copy-start
  0.6 1.4 %copy.8.e_ref = bf16[64,32]{1,0:T(8,128)(2,1)} copy(bf16[64,32]{0,1:T(8,128)(2,1)} %param.8) | data formatting | bytes 8192 | tf_op args[3]
  2.0 0.0 copy-done
  2.0 0.7 %copy.7.l_ref = bf16[128,32]{1,0:T(8,128)(2,1)} copy(bf16[128,32]{0,1:T(8,128)(2,1)S(1)} %copy-done) | data formatting | bytes 16384 | tf_op args[1]
  2.8 60.8 %shard_map.68 = (f32[128,1024]{1,0:T(8,128)}, f32[128,32]{1,0:T(8,128)}) custom-call(bf16[128,1024]{1,0:T(8,128)(2,1)} %x_ref.1, bf16[128,32]{1,0:T(8,128)(2,1)} %copy.7.l_ref, bf16[64,1024]{1,0:T(8,128)(2,1)} %g_ref.1, bf16[64,32]{1,0:T(8,128)(2,1)} %copy.8.e_ref, f32[1,64]{1,0:T(1,128)} %bitcast.1), custom_call_target="tpu_custom_call" | custom-call | tf_op jit(solution)/shard_map/pallas_call | solution.py:236
  63.5 1.5 %copy.9 = f32[128,32]{0,1:T(8,128)} copy(f32[128,32]{1,0:T(8,128)} %get-tuple-element.3) | data formatting | bytes 32768 | tf_op jit(solution)/shard_map/pallas_call | solution.py:236
  65.0 1.9 %copy.11 = f32[128,1024]{1,0:T(8,128)} copy(f32[128,1024]{1,0:T(8,128)} %get-tuple-element.6) | data formatting | bytes 1048576
Async XLA Ops:
  0.6 1.4 %copy-start = (bf16[128,32]{0,1:T(8,128)(2,1)S(1)}, bf16[128,32]{0,1:T(8,128)(2,1)}, u32[]{:S(2)}) copy-start(bf16[128,32]{0,1:T(8,128)(2,1)} %param.6) | copy-start | bytes 24580

commit v2 on v1

v2 whole, which is shorter than its diff:
```python
import functools
import math

import jax
import jax.numpy as jnp
from jax import lax
from jax.experimental import pallas as pl
from jax.experimental.pallas import tpu as pltpu
from jax.sharding import PartitionSpec as P

MESH = pl.DeviceIdType.MESH
F32 = jnp.float32
BF16 = jnp.bfloat16
LAST = (((1,), (1,)), ((), ()))
PLANE = (
    (0, 0), (1, 0), (0, 1), (3, 0), (0, 3), (1, 1), (3, 3), (3, 1), (1, 3),
    (2, 0), (0, 2), (2, 1), (1, 2), (2, 3), (3, 2), (2, 2),
)
EARLY = 4
PASS = 512


def coordinates():
    lm, node = lax.axis_index("lm"), lax.axis_index("node")
    return (lm // 8) + 2 * (node // 8), (node // 2) % 4, lm % 8, node % 2


def device(x, y, z, core):
    return {"lm": (x % 2) * 8 + z, "node": (x // 2 * 4 + y) * 2 + core}


def pieces(rows, ones_first):
    square = jnp.sum(rows * rows, axis=1, keepdims=True) * -0.5
    high = square.astype(BF16).astype(F32)
    rest = square - high
    middle = rest.astype(BF16).astype(F32)
    low = rest - middle
    lane = lax.broadcasted_iota(jnp.int32, rows.shape, 1)
    at = 3 if ones_first else 0
    one = 0 if ones_first else 3
    zero = jnp.zeros(rows.shape, F32)
    out = jnp.where((lane >= one) & (lane < one + 3), 1.0, zero)
    out = jnp.where(lane == at, high, out)
    out = jnp.where(lane == at + 1, middle, out)
    out = jnp.where(lane == at + 2, low, out)
    return out.astype(BF16)


def kernel(
    factor, x_ref, l_ref, g_ref, e_ref, inv_ref, gf_ref, gl_ref,
    marks, mate_x, mate_g, far_x, far_g, cross_x, cross_g, rows, grads, wide, weights,
    send1, recv1, own, send3, recv3, part, mate_part, send4, recv4, back, mate_back, mine,
    z_s, z_r, c_s, c_r, g_s, g_r, r1_s, r1_r, r3_s, r3_r, t_s, t_r,
):
    x, y, z, core = coordinates()
    half = x_ref.shape[1]
    level = z // 2
    chip = 2 * half

    def in_plane(i, sign):
        return device((x + 4 + sign * PLANE[i][0]) % 4, (y + 4 + sign * PLANE[i][1]) % 4, z, core)

    def on_z(step):
        return device(x, y, (z + 2 * step) % 8, core)

    mate = device(x, y, z, 1 - core)
    far = device(x, y, z + 1 - 2 * (z % 2), core)

    def remote(src, dst, s, r, to):
        return pltpu.make_async_remote_copy(
            src_ref=src, dst_ref=dst, send_sem=s, recv_sem=r, device_id=to, device_id_type=MESH
        )

    barrier = pltpu.get_barrier_semaphore()
    partners = [on_z(d) for d in range(1, 4)] + [in_plane(i, 1) for i in range(1, 16)] + [mate, far]
    for partner in partners:
        pl.semaphore_signal(barrier, inc=1, device_id=partner, device_id_type=MESH)

    at = pl.ds(pl.multiple_of(level * 16, 16), 16)
    marks[0, 0, at, :] = l_ref[:16, :]
    marks[0, 1, at, :] = l_ref[16:, :]
    projection = e_ref[...].astype(F32) * inv_ref[...]
    marks[0, 2, at, :] = jnp.concatenate([projection[:16], projection[16:]], axis=1).astype(BF16)

    pl.semaphore_wait(barrier, len(partners))
    sent = []

    def go(copy):
        copy.start()
        sent.append(copy)
        return copy

    z_in = [go(remote(marks.at[0, :, at, :], marks.at[0, :, at, :], z_s.at[d], z_r.at[d], on_z(d + 1))) for d in range(3)]
    x_in = go(remote(x_ref, mate_x, c_s.at[0], c_r.at[0], mate))
    g_in = go(remote(g_ref, mate_g, c_s.at[1], c_r.at[1], mate))
    far_in = [
        go(remote(x_ref, far_x, c_s.at[2], c_r.at[2], far)),
        go(remote(g_ref, far_g, c_s.at[3], c_r.at[3], far)),
    ]

    def prepare(x, g, base):
        turned = x[...].astype(F32).T
        rows[base : base + half, :128] = turned.astype(BF16)
        rows[base : base + half, 128:] = pieces(turned, False)
        pulled = g[...].astype(F32).T
        grads[base : base + half, :] = jnp.concatenate([pulled, pulled], axis=1).astype(BF16)
        wide[:128, base : base + half] = x[...]

    prepare(x_ref, g_ref, 0)
    wide[128:, :] = (lax.broadcasted_iota(jnp.int32, (16, 2 * chip), 0) == 0).astype(F32).astype(BF16)
    for c in z_in:
        c.wait_recv()
    incoming = {}
    for i in range(1, 16):
        incoming[i] = go(remote(marks.at[0], marks.at[i], g_s.at[i], g_r.at[i], in_plane(i, -1)))
    x_in.wait_recv()
    g_in.wait_recv()
    prepare(mate_x, mate_g, half)

    scale = factor * math.log2(math.e)

    def mark_rows(p):
        return marks[2 * p : 2 * p + 2, 0:2].reshape(256, 128)

    def weigh(p, base):
        plain = mark_rows(p)
        near = jnp.concatenate([plain, pieces(plain.astype(F32), True)], axis=1)
        pull = []
        for i in (2 * p, 2 * p + 1):
            packed = marks[i, 2]
            lane = lax.broadcasted_iota(jnp.int32, packed.shape, 1)
            zero = jnp.zeros_like(packed)
            pull += [jnp.where(lane < 64, packed, zero), jnp.where(lane < 64, zero, packed)]
        pull = jnp.concatenate(pull, axis=0)
        cross = lax.dot_general(rows[base : base + chip, :], near, LAST, preferred_element_type=F32)
        pulled = lax.dot_general(grads[base : base + chip, :], pull, LAST, preferred_element_type=F32)
        weights[p, base : base + chip, :] = (pulled * jnp.exp2(cross * scale)).astype(BF16)

    def backward(p):
        total = jnp.dot(wide[...], weights[p], preferred_element_type=F32).T
        return total[:, :128] - mark_rows(p).astype(F32) * total[:, 128:129]

    reduce1 = {}

    def finish(p):
        total = backward(p)
        for i in (2 * p, 2 * p + 1):
            block = total[(i % 2) * 128 : (i % 2) * 128 + 128]
            if i:
                send1[i] = block.astype(BF16)
            else:
                own[...] = block

    def ship(p):
        for i in (2 * p, 2 * p + 1):
            if i:
                reduce1[i] = go(remote(send1.at[i], recv1.at[i], r1_s.at[i], r1_r.at[i], in_plane(i, 1)))

    def arrived(p):
        for i in (2 * p, 2 * p + 1):
            if i:
                incoming[i].wait_recv()

    for p in range(EARLY):
        arrived(p)
        weigh(p, 0)
    for c in far_in:
        c.wait_recv()
    cross_in = [
        go(remote(far_x, cross_x, c_s.at[4], c_r.at[4], mate)),
        go(remote(far_g, cross_g, c_s.at[5], c_r.at[5], mate)),
    ]
    prepare(far_x, far_g, chip)
    arrived(EARLY)
    weigh(EARLY, 0)
    for c in cross_in:
        c.wait_recv()
    prepare(cross_x, cross_g, chip + half)
    for p in range(EARLY + 1):
        weigh(p, chip)
        if p:
            finish(p - 1)
    for p in range(EARLY):
        ship(p)
    for p in range(EARLY + 1, 8):
        arrived(p)
        weigh(p, 0)
        finish(p - 1)
        weigh(p, chip)
        ship(p - 1)
    finish(7)
    ship(7)

    ones = (lax.broadcasted_iota(jnp.int32, (256, 128), 1) == 0).astype(F32).astype(BF16)

    def toward(r):
        total = jnp.zeros((PASS, 256), F32)
        for p in range(8):
            total = total + jnp.dot(
                weights[p, r : r + PASS, :], jnp.concatenate([mark_rows(p), ones], axis=1), preferred_element_type=F32
            )
        return total[:, :128] - rows[r : r + PASS, :128].astype(F32) * total[:, 128:129]

    for r in range(0, half, PASS):
        part[r : r + PASS, :] = toward(chip + half + r)
    part_in = go(remote(part, mate_part, t_s.at[0], t_r.at[0], mate))
    for r in range(0, half, PASS):
        mine[r : r + PASS, :] = toward(chip + r)
    part_in.wait_recv()
    send4[...] = (mine[...] + mate_part[...]).astype(BF16)
    far_back = go(remote(send4, recv4, t_s.at[1], t_r.at[1], far))

    for i in range(1, 16):
        reduce1[i].wait_recv()
    total = own[...]
    for i in range(1, 16):
        total = total + recv1[i].astype(F32)
    send3[...] = total.reshape(2, 64, 128)
    reduce3 = []
    for d in range(3):
        to = pl.ds(pl.multiple_of((level + d + 1) % 4 * 16, 16), 16)
        reduce3.append(go(remote(send3.at[:, to, :], recv3.at[d], r3_s.at[d], r3_r.at[d], on_z(d + 1))))

    for r in range(0, half, PASS):
        back[r : r + PASS, :] = toward(half + r)
    t_in = go(remote(back, mate_back, t_s.at[2], t_r.at[2], mate))
    for r in range(0, half, PASS):
        mine[r : r + PASS, :] = toward(r)

    for c in reduce3:
        c.wait_recv()
    total = send3[:, at, :]
    for d in range(3):
        total = total + recv3[d]
    gl_ref[...] = factor * total.reshape(32, 128)
    t_in.wait_recv()
    far_back.wait_recv()
    gf_ref[...] = factor * (mine[...] + mate_back[...] + recv4[...].astype(F32)).T
    for c in sent:
        c.wait_send()


def per_device(features, landmarks, cotangent, eigen_basis, inv_eigen):
    width, count = features.shape
    vmem = pl.BlockSpec(memory_space=pltpu.VMEM)
    dma = pltpu.SemaphoreType.DMA
    grad_features, grad_landmarks = pl.pallas_call(
        functools.partial(kernel, 4.0 / width),
        out_shape=(
            jax.ShapeDtypeStruct(features.shape, F32),
            jax.ShapeDtypeStruct(landmarks.shape[::-1], F32),
        ),
        in_specs=[vmem] * 5,
        out_specs=(vmem, vmem),
        scratch_shapes=[
            pltpu.VMEM((16, 3, 64, 128), BF16),
            pltpu.VMEM((128, count), BF16),
            pltpu.VMEM((64, count), BF16),
            pltpu.VMEM((128, count), BF16),
            pltpu.VMEM((64, count), BF16),
            pltpu.VMEM((128, count), BF16),
            pltpu.VMEM((64, count), BF16),
            pltpu.VMEM((4 * count, 256), BF16),
            pltpu.VMEM((4 * count, 128), BF16),
            pltpu.VMEM((144, 4 * count), BF16),
            pltpu.VMEM((8, 4 * count, 256), BF16),
            pltpu.VMEM((16, 128, 128), BF16),
            pltpu.VMEM((16, 128, 128), BF16),
            pltpu.VMEM((128, 128), F32),
            pltpu.VMEM((2, 64, 128), F32),
            pltpu.VMEM((3, 2, 16, 128), F32),
            pltpu.VMEM((count, 128), F32),
            pltpu.VMEM((count, 128), F32),
            pltpu.VMEM((count, 128), BF16),
            pltpu.VMEM((count, 128), BF16),
            pltpu.VMEM((count, 128), F32),
            pltpu.VMEM((count, 128), F32),
            pltpu.VMEM((count, 128), F32),
            dma((3,)), dma((3,)), dma((6,)), dma((6,)), dma((16,)), dma((16,)),
            dma((16,)), dma((16,)), dma((3,)), dma((3,)), dma((3,)), dma((3,)),
        ],
        compiler_params=pltpu.CompilerParams(
            collective_id=0, has_side_effects=True, vmem_limit_bytes=60 * 2**20
        ),
    )(features, landmarks.T, cotangent, eigen_basis.T, inv_eigen.reshape(1, -1))
    return grad_features, grad_landmarks.T


def solution(mesh):
    return jax.shard_map(
        per_device,
        mesh=mesh,
        in_specs=(
            P(None, ("node", "lm")),
            P(None, ("lm", "node")),
            P(None, ("node", "lm")),
            P(None, ("lm", "node")),
            P(),
        ),
        out_specs=(P(None, ("node", "lm")), P(None, ("lm", "node"))),
        check_vma=False,
    )
```

time: 67.2 us -> 55.9 us (0.83)
  the two profiles are of different devices: /device:TPU:6 before, /device:TPU:1 now
where the time goes in v2:
time: 55.9 us; the launch traced here: 55.8 us
  Pallas kernels  52.6 us (94%)
  local copies, waits for them, and re-layouts  2.5 us (4%)
  between operations  0.65 us (1%)
    pallas_call x1, Pallas kernels, per_device(): pl.pallas_call(functools.partial(kernel, 4.0 / width), out_shape=(jax.Sha...  52.6 us
    unnamed x4, local copies, waits for them, and re-layouts  2.5 us

profile of v2, /device:TPU:1, one launch (start us, length us, event | category | flops | bytes accessed | tf_op | source)
XLA Modules:
  0.0 55.8 jit_solution(8325952466593231822)
XLA Ops:
  0.6 52.6 %shard_map.68 = (f32[128,1024]{1,0:T(8,128)}, f32[32,128]{1,0:T(8,128)}) custom-call(bf16[128,1024]{1,0:T(8,128)(2,1)} %x_ref.1, bf16[32,128]{1,0:T(8,128)(2,1)} %bitcast.5, bf16[64,1024]{1,0:T(8,128)(2,1)} %g_ref.1, bf16[32,64]{1,0:T(8,128)(2,1)} %bitcast.6, f32[1,64]{1,0:T(1,128)} %bitcast.7), custom_call_target="tpu_custom_call" | custom-call | tf_op jit(solution)/shard_map/pallas_call | solution.py:247
  53.3 0.0 copy-start
  53.3 1.9 %copy.9 = f32[128,1024]{1,0:T(8,128)} copy(f32[128,1024]{1,0:T(8,128)} %get-tuple-element.8) | data formatting | bytes 1048576
  55.2 0.0 copy-done
  55.2 0.6 %copy.10 = f32[128,32]{0,1:T(8,128)} copy(f32[128,32]{0,1:T(8,128)S(1)} %bitcast.4) | data formatting | bytes 32768
Async XLA Ops:
  53.3 1.9 %copy-start = (f32[32,128]{1,0:T(8,128)S(1)}, f32[32,128]{1,0:T(8,128)}, u32[]{:S(2)}) copy-start(f32[32,128]{1,0:T(8,128)} %get-tuple-element.5) | copy-start | bytes 49156

commit v3 on v2

--- a/solution.py
+++ b/solution.py
@@ -16,7 +16,6 @@
     (0, 0), (1, 0), (0, 1), (3, 0), (0, 3), (1, 1), (3, 3), (3, 1), (1, 3),
     (2, 0), (0, 2), (2, 1), (1, 2), (2, 3), (3, 2), (2, 2),
 )
-EARLY = 4
 PASS = 512
 
 
@@ -111,11 +110,16 @@
     for c in z_in:
         c.wait_recv()
     incoming = {}
-    for i in range(1, 16):
-        incoming[i] = go(remote(marks.at[0], marks.at[i], g_s.at[i], g_r.at[i], in_plane(i, -1)))
+
+    def offer(*blocks):
+        for i in blocks:
+            incoming[i] = go(remote(marks.at[0], marks.at[i], g_s.at[i], g_r.at[i], in_plane(i, -1)))
+
+    offer(1, 2, 3, 4)
     x_in.wait_recv()
     g_in.wait_recv()
     prepare(mate_x, mate_g, half)
+    offer(5, 6, 7, 8)
 
     scale = factor * math.log2(math.e)
 
@@ -161,36 +165,6 @@
             if i:
                 incoming[i].wait_recv()
 
-    for p in range(EARLY):
-        arrived(p)
-        weigh(p, 0)
-    for c in far_in:
-        c.wait_recv()
-    cross_in = [
-        go(remote(far_x, cross_x, c_s.at[4], c_r.at[4], mate)),
-        go(remote(far_g, cross_g, c_s.at[5], c_r.at[5], mate)),
-    ]
-    prepare(far_x, far_g, chip)
-    arrived(EARLY)
-    weigh(EARLY, 0)
-    for c in cross_in:
-        c.wait_recv()
-    prepare(cross_x, cross_g, chip + half)
-    for p in range(EARLY + 1):
-        weigh(p, chip)
-        if p:
-            finish(p - 1)
-    for p in range(EARLY):
-        ship(p)
-    for p in range(EARLY + 1, 8):
-        arrived(p)
-        weigh(p, 0)
-        finish(p - 1)
-        weigh(p, chip)
-        ship(p - 1)
-    finish(7)
-    ship(7)
-
     ones = (lax.broadcasted_iota(jnp.int32, (256, 128), 1) == 0).astype(F32).astype(BF16)
 
     def toward(r):
@@ -201,14 +175,74 @@
             )
         return total[:, :128] - rows[r : r + PASS, :128].astype(F32) * total[:, 128:129]
 
+    arrived(0)
+    arrived(1)
+    offer(9, 10, 11)
+    weigh(0, 0)
+    weigh(1, 0)
+    arrived(2)
+    arrived(3)
+    offer(12, 13, 14, 15)
+    weigh(2, 0)
+    weigh(3, 0)
+    for c in far_in:
+        c.wait_recv()
+    cross_in = [
+        go(remote(far_x, cross_x, c_s.at[4], c_r.at[4], mate)),
+        go(remote(far_g, cross_g, c_s.at[5], c_r.at[5], mate)),
+    ]
+    arrived(4)
+    prepare(far_x, far_g, chip)
+    weigh(4, 0)
+    for c in cross_in:
+        c.wait_recv()
+    prepare(cross_x, cross_g, chip + half)
+    for p in range(4):
+        weigh(p, chip)
+        if p:
+            finish(p - 1)
+    for p in range(3):
+        ship(p)
+    arrived(5)
+    weigh(4, chip)
+    finish(3)
+    weigh(5, 0)
+    finish(4)
+    weigh(5, chip)
+    ship(3)
+    ship(4)
+    arrived(6)
+    arrived(7)
+    weigh(6, 0)
+    finish(5)
+    weigh(6, chip)
+    weigh(7, 0)
+    finish(6)
+    weigh(7, chip)
+    ship(5)
+    ship(6)
+    finish(7)
+    ship(7)
+
+    part_in = []
+    for n in range(2):
+        r = pl.ds(n * PASS, PASS)
+        part[r, :] = toward(chip + half + n * PASS)
+        part_in.append(go(remote(part.at[r, :], mate_part.at[r, :], t_s.at[n], t_r.at[n], mate)))
+    far_back = []
+
+    def send_back(n):
+        r = pl.ds(n * PASS, PASS)
+        part_in[n].wait_recv()
+        send4[r, :] = (mine[r, :] + mate_part[r, :]).astype(BF16)
+        far_back.append(go(remote(send4.at[r, :], recv4.at[r, :], t_s.at[2 + n], t_r.at[2 + n], far)))
+
+    mine[:PASS, :] = toward(chip)
+    send_back(0)
+    mine[PASS:, :] = toward(chip + PASS)
     for r in range(0, half, PASS):
-        part[r : r + PASS, :] = toward(chip + half + r)
-    part_in = go(remote(part, mate_part, t_s.at[0], t_r.at[0], mate))
-    for r in range(0, half, PASS):
-        mine[r : r + PASS, :] = toward(chip + r)
-    part_in.wait_recv()
-    send4[...] = (mine[...] + mate_part[...]).astype(BF16)
-    far_back = go(remote(send4, recv4, t_s.at[1], t_r.at[1], far))
+        back[r : r + PASS, :] = toward(half + r)
+    t_in = go(remote(back, mate_back, t_s.at[4], t_r.at[4], mate))
 
     for i in range(1, 16):
         reduce1[i].wait_recv()
@@ -220,10 +254,8 @@
     for d in range(3):
         to = pl.ds(pl.multiple_of((level + d + 1) % 4 * 16, 16), 16)
         reduce3.append(go(remote(send3.at[:, to, :], recv3.at[d], r3_s.at[d], r3_r.at[d], on_z(d + 1))))
-
-    for r in range(0, half, PASS):
-        back[r : r + PASS, :] = toward(half + r)
-    t_in = go(remote(back, mate_back, t_s.at[2], t_r.at[2], mate))
+    send_back(1)
+
     for r in range(0, half, PASS):
         mine[r : r + PASS, :] = toward(r)
 
@@ -234,7 +266,8 @@
         total = total + recv3[d]
     gl_ref[...] = factor * total.reshape(32, 128)
     t_in.wait_recv()
-    far_back.wait_recv()
+    for c in far_back:
+        c.wait_recv()
     gf_ref[...] = factor * (mine[...] + mate_back[...] + recv4[...].astype(F32)).T
     for c in sent:
         c.wait_send()
@@ -277,7 +310,7 @@
             pltpu.VMEM((count, 128), F32),
             pltpu.VMEM((count, 128), F32),
             dma((3,)), dma((3,)), dma((6,)), dma((6,)), dma((16,)), dma((16,)),
-            dma((16,)), dma((16,)), dma((3,)), dma((3,)), dma((3,)), dma((3,)),
+            dma((16,)), dma((16,)), dma((3,)), dma((3,)), dma((5,)), dma((5,)),
         ],
         compiler_params=pltpu.CompilerParams(
             collective_id=0, has_side_effects=True, vmem_limit_bytes=60 * 2**20

time: 55.9 us -> 53.9 us (0.964)
  Pallas kernels: 52.6 us -> 50.7 us
    pallas_call x1, Pallas kernels: 52.6 us -> 50.7 us  [per_device(): pl.pallas_call(functools.partial(kernel, 4.0 / width), out_shape=(jax.Sha...]
where the time goes in v3:
time: 53.9 us; the launch traced here: 53.8 us
  Pallas kernels  50.7 us (94%)
  local copies, waits for them, and re-layouts  2.5 us (5%)
  between operations  0.65 us (1%)
    pallas_call x1, Pallas kernels, per_device(): pl.pallas_call(functools.partial(kernel, 4.0 / width), out_shape=(jax.Sha...  50.7 us
    unnamed x4, local copies, waits for them, and re-layouts  2.5 us

profile of v3, /device:TPU:1, one launch (start us, length us, event | category | flops | bytes accessed | tf_op | source)
XLA Modules:
  0.0 53.8 jit_solution(5138922360394328499)
XLA Ops:
  0.6 50.7 %shard_map.68 = (f32[128,1024]{1,0:T(8,128)}, f32[32,128]{1,0:T(8,128)}) custom-call(bf16[128,1024]{1,0:T(8,128)(2,1)} %x_ref.1, bf16[32,128]{1,0:T(8,128)(2,1)} %bitcast.5, bf16[64,1024]{1,0:T(8,128)(2,1)} %g_ref.1, bf16[32,64]{1,0:T(8,128)(2,1)} %bitcast.6, f32[1,64]{1,0:T(1,128)} %bitcast.7), custom_call_target="tpu_custom_call" | custom-call | tf_op jit(solution)/shard_map/pallas_call | solution.py:280
  51.3 0.0 copy-start
  51.3 1.9 %copy.9 = f32[128,1024]{1,0:T(8,128)} copy(f32[128,1024]{1,0:T(8,128)} %get-tuple-element.8) | data formatting | bytes 1048576
  53.2 0.0 copy-done
  53.2 0.6 %copy.10 = f32[128,32]{0,1:T(8,128)} copy(f32[128,32]{0,1:T(8,128)S(1)} %bitcast.4) | data formatting | bytes 32768
Async XLA Ops:
  51.3 1.9 %copy-start = (f32[32,128]{1,0:T(8,128)S(1)}, f32[32,128]{1,0:T(8,128)}, u32[]{:S(2)}) copy-start(f32[32,128]{1,0:T(8,128)} %get-tuple-element.5) | copy-start | bytes 49156

commit v4 on v3

--- a/solution.py
+++ b/solution.py
@@ -180,20 +180,18 @@
     offer(9, 10, 11)
     weigh(0, 0)
     weigh(1, 0)
+    for c in far_in:
+        c.wait_recv()
+    cross_in = [
+        go(remote(far_x, cross_x, c_s.at[4], c_r.at[4], mate)),
+        go(remote(far_g, cross_g, c_s.at[5], c_r.at[5], mate)),
+    ]
+    prepare(far_x, far_g, chip)
     arrived(2)
     arrived(3)
     offer(12, 13, 14, 15)
     weigh(2, 0)
     weigh(3, 0)
-    for c in far_in:
-        c.wait_recv()
-    cross_in = [
-        go(remote(far_x, cross_x, c_s.at[4], c_r.at[4], mate)),
-        go(remote(far_g, cross_g, c_s.at[5], c_r.at[5], mate)),
-    ]
-    arrived(4)
-    prepare(far_x, far_g, chip)
-    weigh(4, 0)
     for c in cross_in:
         c.wait_recv()
     prepare(cross_x, cross_g, chip + half)
@@ -203,9 +201,11 @@
             finish(p - 1)
     for p in range(3):
         ship(p)
+    arrived(4)
     arrived(5)
+    weigh(4, 0)
+    finish(3)
     weigh(4, chip)
-    finish(3)
     weigh(5, 0)
     finish(4)
     weigh(5, chip)

time: 53.9 us -> 52.1 us (0.967)
  Pallas kernels: 50.7 us -> 48.9 us
    pallas_call x1, Pallas kernels: 50.7 us -> 48.9 us  [per_device(): pl.pallas_call(functools.partial(kernel, 4.0 / width), out_shape=(jax.Sha...]
where the time goes in v4:
time: 52.1 us; the launch traced here: 52 us
  Pallas kernels  48.9 us (94%)
  local copies, waits for them, and re-layouts  2.5 us (5%)
  between operations  0.65 us (1%)
    pallas_call x1, Pallas kernels, per_device(): pl.pallas_call(functools.partial(kernel, 4.0 / width), out_shape=(jax.Sha...  48.9 us
    unnamed x4, local copies, waits for them, and re-layouts  2.5 us

profile of v4, /device:TPU:1, one launch (start us, length us, event | category | flops | bytes accessed | tf_op | source)
XLA Modules:
  0.0 52.0 jit_solution(17319991954587226564)
XLA Ops:
  0.6 48.9 %shard_map.68 = (f32[128,1024]{1,0:T(8,128)}, f32[32,128]{1,0:T(8,128)}) custom-call(bf16[128,1024]{1,0:T(8,128)(2,1)} %x_ref.1, bf16[32,128]{1,0:T(8,128)(2,1)} %bitcast.5, bf16[64,1024]{1,0:T(8,128)(2,1)} %g_ref.1, bf16[32,64]{1,0:T(8,128)(2,1)} %bitcast.6, f32[1,64]{1,0:T(1,128)} %bitcast.7), custom_call_target="tpu_custom_call" | custom-call | tf_op jit(solution)/shard_map/pallas_call | solution.py:280
  49.5 0.0 copy-start
  49.5 1.9 %copy.9 = f32[128,1024]{1,0:T(8,128)} copy(f32[128,1024]{1,0:T(8,128)} %get-tuple-element.8) | data formatting | bytes 1048576
  51.4 0.0 copy-done
  51.4 0.6 %copy.10 = f32[128,32]{0,1:T(8,128)} copy(f32[128,32]{0,1:T(8,128)S(1)} %bitcast.4) | data formatting | bytes 32768
Async XLA Ops:
  49.5 1.9 %copy-start = (f32[32,128]{1,0:T(8,128)S(1)}, f32[32,128]{1,0:T(8,128)}, u32[]{:S(2)}) copy-start(f32[32,128]{1,0:T(8,128)} %get-tuple-element.5) | copy-start | bytes 49156
